TPU v7x, 256 devices: a whole 4x4x8 slice. The times are simulated.
256 devices in a mesh: slab: 32 (over x, z_hi, core), blk: 8 (over z_lo, y).
Axes of the slice: x: 4, y: 4, z: 8 (z_hi: 4, z_lo: 2; z = z_hi * 2 + z_lo), core: 2. Of those that a mesh axis runs over, the one named last changes fastest.
Arguments:
- vectors: bfloat16 [147456, 3072], P('slab', 'blk'), may hold values from -0.25 to 0.25
- state_order: int32 [3072], P('blk'), may hold values from 0 to 383, as said below
Outputs:
- currents: float32 [4, 384, 3072], P(None, 'slab', 'blk')
Inputs may be any that keep to these rules, and one draw needn't show every extreme that they name: `state_order`: each aligned run of 384 entries holds every number from 0 to 383 exactly once.
All inputs are finite; a program needn't handle non-finite values.
Results may differ from a plain program's by a relative error of at most 0.0031.
Values may be sent and summed in bfloat16 or wider, within the bound.
A program may use at most 128 MiB of HBM per device.

v0:
```python
import jax
import jax.numpy as jnp
from jax import lax
from jax.sharding import PartitionSpec as P

LX = 48
LY = 48
WINDOW = 4


def padded_2(array, sides, width):
    for axis, dim in sides:
        count, length = (lax.axis_size(axis), array.shape[dim])
        up = [(i, (i + 1) % count) for i in range(count)]
        down = [(j, i) for i, j in up]
        last = lax.slice_in_dim(array, length - width, length, axis=dim)
        initial = lax.slice_in_dim(array, 0, width, axis=dim)
        before = lax.ppermute(last, axis, up)
        after = lax.ppermute(initial, axis, down)
        array = jnp.concatenate([before, array, after], axis=dim)
    return array


def passed_along(array, axis, by):
    count = lax.axis_size(axis)
    return lax.ppermute(array, axis, [(i, (i + by) % count) for i in range(count)])


def apply_current(field_block):
    padded = padded_2(field_block, (("slab", 0),), 1)
    upper_plane = padded[2:].astype(jnp.float32)
    lower_plane = padded[:-2].astype(jnp.float32)
    return (upper_plane - lower_plane).astype(jnp.bfloat16)


def pass_on(field_block):
    return passed_along(field_block, "blk", -1)


def partial_term(image_flat, own_flat):
    return lax.dot_general(
        image_flat, own_flat, (((0,), (0,)), ((), ())), preferred_element_type=jnp.float32
    )


def on_device(vectors, state_order):
    row_count, col_count = vectors.shape
    plane_count = row_count // (LX * LY)
    step_count = min(WINDOW, lax.axis_size("blk"))
    sorted_vec = jnp.take(vectors, state_order, axis=1)
    own_block = sorted_vec.reshape(plane_count, LX * LY, col_count)
    image_list = []
    moving = apply_current(own_block)
    for turn_index in range(step_count):
        if turn_index > 0:
            moving = pass_on(moving)
        image_list.append(moving.reshape(row_count, col_count))

    def term_for(image_flat):
        return partial_term(image_flat, sorted_vec)

    results = [
        lax.psum_scatter(term_for(image_flat), "slab", scatter_dimension=0, tiled=True)
        for image_flat in image_list
    ]
    return jnp.stack(results, axis=0)


def solution(mesh):
    return jax.shard_map(
        on_device,
        mesh=mesh,
        in_specs=(P("slab", "blk"), P("blk")),
        out_specs=P(None, "slab", "blk"),
        check_vma=False,
    )
```

profile of v0, /device:TPU:1, one launch (start us, length us, event | category | flops | bytes accessed | tf_op | source)
XLA Modules:
  0.0 513.1 jit_solution(2269674132804330922)
XLA Ops:
  1.4 4.3 copy.7
  5.7 4.5 gather_fusion
  10.2 2.4 broadcast_select_fusion.1
  12.6 2.1 slice_bitcast_fusion.1
  14.7 1.4 copy-done.1
  16.1 3.2 collective-permute-start
  20.5 3.1 gather.7
  23.6 5.4 %broadcast_select_fusion = bf16[2,2304,384]{1,0,2:T(2,128)(2,1)S(1)} fusion(bf16[2,2304,384]{1,0,2:T(2,128)(2,1)} %gather.7, pred[384]{0:T(512)(128)(4,1)S(1)} %compare_and_fusion), kind=kLoop, calls=%fused_computation.2 | loop fusion | flops 1769472 | bytes 7078272 | tf_op jit(solution)/shard_map/jit(_take)/select_n | solution.py:50
  29.0 31.3 %collective-permute-done = bf16[1,2304,384]{1,2,0:T(8,128)(2,1)} collective-permute-done((bf16[1,2304,384]{1,2,0:T(8,128)(2,1)}, bf16[1,2304,384]{1,2,0:T(8,128)(2,1)}, u32[]{:S(2)}, u32[]{:S(2)}) %collective-permute-start) | collective-permute-done | bytes 1769504 | tf_op jit(solution)/shard_map/ppermute | solution.py:19
  60.3 4.2 copy.8
  64.5 4.2 copy.9
  68.7 15.7 %subtract_convert_fusion = bf16[2,2304,384]{1,0,2:T(2,128)(2,1)S(1)} fusion(bf16[2,2304,384]{1,0,2:T(2,128)(2,1)S(1)} %broadcast_select_fusion, bf16[1,2304,384]{1,0,2:T(2,128)(2,1)S(1)} %copy.9, bf16[1,2304,384]{1,0,2:T(2,128)(2,1)S(1)} %copy.8), kind=kLoop, calls=%fused_computation.1 | loop fusion | flops 17694720 | bytes 10616832 | tf_op jit(solution)/shard_map/convert_element_type | solution.py:33
  84.8 72.5 %collective-permute-done.2 = bf16[2,2304,384]{1,0,2:T(2,128)(2,1)S(1)} collective-permute-done((bf16[2,2304,384]{1,0,2:T(2,128)(2,1)S(1)}, bf16[2,2304,384]{1,0,2:T(2,128)(2,1)S(1)}, u32[]{:S(2)}, u32[]{:S(2)}) %collective-permute-start.2) | collective-permute-done | bytes 3538976 | tf_op jit(solution)/shard_map/ppermute | solution.py:26
  157.3 75.0 %collective-permute-done.3 = bf16[2,2304,384]{1,0,2:T(2,128)(2,1)S(1)} collective-permute-done((bf16[2,2304,384]{1,0,2:T(2,128)(2,1)S(1)}, bf16[2,2304,384]{1,0,2:T(2,128)(2,1)S(1)}, u32[]{:S(2)}, u32[]{:S(2)}) %collective-permute-start.3) | collective-permute-done | bytes 3538976 | tf_op jit(solution)/shard_map/ppermute | solution.py:26
  232.8 1.5 copy-done.2
  234.3 2.0 fusion.5
  236.8 2.0 fusion.6
  239.3 2.0 fusion.7
  241.3 66.0 %collective-permute-done.4 = bf16[2,2304,384]{1,0,2:T(2,128)(2,1)S(1)} collective-permute-done((bf16[2,2304,384]{1,0,2:T(2,128)(2,1)S(1)}, bf16[2,2304,384]{1,0,2:T(2,128)(2,1)S(1)}, u32[]{:S(2)}, u32[]{:S(2)}) %collective-permute-start.4) | collective-permute-done | bytes 3538976 | tf_op jit(solution)/shard_map/ppermute | solution.py:26
  307.8 2.0 fusion.8
  309.8 102.8 %fusion.4 = (f32[16,384]{1,0:T(8,128)S(1)}, f32[16,384]{1,0:T(8,128)S(1)}, f32[16,384]{1,0:T(8,128)S(1)}, f32[16,384]{1,0:T(8,128)S(1)}) fusion(f32[384,384]{1,0:T(8,128)S(1)} %fusion.8, f32[384,384]{1,0:T(8,128)S(1)} %fusion.7, f32[384,384]{1,0:T(8,128)S(1)} %fusion.6, f32[384,384]{1,0:T(8,128)S(1)} %fusion.5), kind=kCustom, calls=%all-reduce-scatter.4 | all-reduce-scatter fusion | flops 786433 | bytes 2458624
  412.6 1.3 collective-permute-start.20
  413.9 1.3 collective-permute-start.28
  415.2 2.4 collective-permute-start.35
  417.6 5.0 collective-permute-start.34
  423.9 10.5 %collective-permute-start.32 = (f32[16,384]{1,0:T(8,128)S(1)}, f32[16,384]{1,0:T(8,128)S(1)}, u32[]{:S(2)}, u32[]{:S(2)}) collective-permute-start(f32[16,384]{1,0:T(8,128)S(1)} %get-tuple-element.9), channel_id=1, source_target_pairs={{0,32},{8,40},{16,48},{24,56},{32,64},{40,72},{48,80},{56,88},{64,... | collective-permute-start | bytes 73736
  434.4 1.3 collective-permute-start.36
  436.7 3.4 collective-permute-start.31
  440.1 4.0 collective-permute-start.30
  444.1 1.9 collective-permute-start.29
  446.0 4.3 collective-permute-start.27
  450.4 2.9 collective-permute-start.26
  453.3 5.3 %collective-permute-start.25 = (f32[16,384]{1,0:T(8,128)S(1)}, f32[16,384]{1,0:T(8,128)S(1)}, u32[]{:S(2)}, u32[]{:S(2)}) collective-permute-start(f32[16,384]{1,0:T(8,128)S(1)} %get-tuple-element.10), channel_id=1, source_target_pairs={{0,40},{8,48},{16,56},{24,64},{32,72},{40,80},{48,88},{56,96},{64,... | collective-permute-start | bytes 73736
  458.5 3.6 collective-permute-start.24
  462.2 5.3 %collective-permute-start.23 = (f32[16,384]{1,0:T(8,128)S(1)}, f32[16,384]{1,0:T(8,128)S(1)}, u32[]{:S(2)}, u32[]{:S(2)}) collective-permute-start(f32[16,384]{1,0:T(8,128)S(1)} %get-tuple-element.10), channel_id=1, source_target_pairs={{0,24},{8,32},{16,40},{24,48},{32,56},{40,64},{48,72},{56,80},{64,... | collective-permute-start | bytes 73736
  467.5 1.3 collective-permute-start.22
  468.8 3.1 collective-permute-start.21
  474.2 1.3 collective-permute-start.19
  475.5 2.5 collective-permute-start.18
  478.0 1.7 collective-permute-start.17
  479.7 2.8 collective-permute-start.16
  482.6 4.4 collective-permute-start.15
  488.0 2.4 collective-permute-start.14
  490.4 2.0 collective-permute-start.13
  497.7 3.3 collective-permute-start.8
  502.0 3.9 collective-permute-start.7
  505.9 2.2 collective-permute-start.6
  508.1 2.5 collective-permute-start.5
  (70 shorter events, 18.3 us)
Async XLA Ops:
  12.6 3.5 copy-start.1
  12.6 7.9 %copy-start = (bf16[384,4608]{1,0:T(8,128)(2,1)S(1)}, bf16[384,4608]{1,0:T(8,128)(2,1)}, u32[]{:S(2)}) copy-start(bf16[384,4608]{1,0:T(8,128)(2,1)} %gather_fusion) | copy-start | bytes 10616836
  16.1 44.2 %collective-permute-start = (bf16[1,2304,384]{1,2,0:T(8,128)(2,1)}, bf16[1,2304,384]{1,2,0:T(8,128)(2,1)}, u32[]{:S(2)}, u32[]{:S(2)}) collective-permute-start(bf16[1,2304,384]{1,2,0:T(8,128)(2,1)} %get-tuple-element.13), channel_id=1, source_target_pairs={{8,0},{16,8},{24,16},{32,24},{40,32},{48,40},{56,48},{64,56},{72,6... | collective-permute-start | bytes 5308424 | tf_op jit(solution)/shard_map/ppermute | solution.py:19
  19.4 45.2 %collective-permute-start.1 = (bf16[1,2304,384]{1,2,0:T(8,128)(2,1)}, bf16[1,2304,384]{1,2,0:T(8,128)(2,1)}, u32[]{:S(2)}, u32[]{:S(2)}) collective-permute-start(bf16[1,2304,384]{1,2,0:T(8,128)(2,1)} %get-tuple-element.14), channel_id=1, source_target_pairs={{0,8},{8,16},{16,24},{24,32},{32,40},{40,48},{48,56},{56,64},{64,7... | collective-permute-start | bytes 5308424 | tf_op jit(solution)/shard_map/ppermute | solution.py:18
  84.5 72.8 %collective-permute-start.2 = (bf16[2,2304,384]{1,0,2:T(2,128)(2,1)S(1)}, bf16[2,2304,384]{1,0,2:T(2,128)(2,1)S(1)}, u32[]{:S(2)}, u32[]{:S(2)}) collective-permute-start(bf16[2,2304,384]{1,0,2:T(2,128)(2,1)S(1)} %subtract_convert_fusion), channel_id=1, source_target_pairs={{0,7},{1,0},{2,1},{3,2},{4,3},{5,4},{6,5},{7,6},{8,15},{9,8},{10,9... | collective-permute-start | bytes 10616840 | tf_op jit(solution)/shard_map/ppermute | solution.py:26
  157.3 75.0 %collective-permute-start.3 = (bf16[2,2304,384]{1,0,2:T(2,128)(2,1)S(1)}, bf16[2,2304,384]{1,0,2:T(2,128)(2,1)S(1)}, u32[]{:S(2)}, u32[]{:S(2)}) collective-permute-start(bf16[2,2304,384]{1,0,2:T(2,128)(2,1)S(1)} %collective-permute-done.2), channel_id=1, source_target_pairs={{0,7},{1,0},{2,1},{3,2},{4,3},{5,4},{6,5},{7,6},{8,15},{9,8},{10,9... | collective-permute-start | bytes 10616840 | tf_op jit(solution)/shard_map/ppermute | solution.py:26
  232.3 75.0 %collective-permute-start.4 = (bf16[2,2304,384]{1,0,2:T(2,128)(2,1)S(1)}, bf16[2,2304,384]{1,0,2:T(2,128)(2,1)S(1)}, u32[]{:S(2)}, u32[]{:S(2)}) collective-permute-start(bf16[2,2304,384]{1,0,2:T(2,128)(2,1)S(1)} %collective-permute-done.3), channel_id=1, source_target_pairs={{0,7},{1,0},{2,1},{3,2},{4,3},{5,4},{6,5},{7,6},{8,15},{9,8},{10,9... | collective-permute-start | bytes 10616840 | tf_op jit(solution)/shard_map/ppermute | solution.py:26
  232.3 2.0 copy-start.2
  307.8 164.2 %copy-start.3 = (u32[256]{0:T(256)S(1)}, u32[256]{0:T(256)}, u32[]{:S(2)}) copy-start(u32[256]{0:T(256)} %constant.18) | copy-start | bytes 3076
  412.6 11.4 %collective-permute-start.20 = (f32[12,384]{1,0:T(8,128)S(1)}, f32[12,384]{1,0:T(8,128)S(1)}, u32[]{:S(2)}, u32[]{:S(2)}) collective-permute-start(f32[12,384]{1,0:T(8,128)S(1)} %slice.31), channel_id=1, source_target_pairs={{0,64},{8,72},{16,80},{24,88},{32,96},{40,104},{48,112},{56,120},{... | collective-permute-start | bytes 55304
  413.9 20.6 %collective-permute-start.28 = (f32[12,384]{1,0:T(8,128)S(1)}, f32[12,384]{1,0:T(8,128)S(1)}, u32[]{:S(2)}, u32[]{:S(2)}) collective-permute-start(f32[12,384]{1,0:T(8,128)S(1)} %slice.32), channel_id=1, source_target_pairs={{0,64},{8,72},{16,80},{24,88},{32,96},{40,104},{48,112},{56,120},{... | collective-permute-start | bytes 55304
  415.2 24.9 %collective-permute-start.35 = (f32[16,384]{1,0:T(8,128)S(1)}, f32[16,384]{1,0:T(8,128)S(1)}, u32[]{:S(2)}, u32[]{:S(2)}) collective-permute-start(f32[16,384]{1,0:T(8,128)S(1)} %get-tuple-element.9), channel_id=1, source_target_pairs={{0,56},{8,64},{16,72},{24,80},{32,88},{40,96},{48,104},{56,112},{6... | collective-permute-start | bytes 73736
  417.6 26.5 %collective-permute-start.34 = (f32[16,384]{1,0:T(8,128)S(1)}, f32[16,384]{1,0:T(8,128)S(1)}, u32[]{:S(2)}, u32[]{:S(2)}) collective-permute-start(f32[16,384]{1,0:T(8,128)S(1)} %get-tuple-element.9), channel_id=1, source_target_pairs={{0,48},{8,56},{16,64},{24,72},{32,80},{40,88},{48,96},{56,104},{64... | collective-permute-start | bytes 73736
  422.6 23.4 %collective-permute-start.33 = (f32[16,384]{1,0:T(8,128)S(1)}, f32[16,384]{1,0:T(8,128)S(1)}, u32[]{:S(2)}, u32[]{:S(2)}) collective-permute-start(f32[16,384]{1,0:T(8,128)S(1)} %get-tuple-element.9), channel_id=1, source_target_pairs={{0,40},{8,48},{16,56},{24,64},{32,72},{40,80},{48,88},{56,96},{64,... | collective-permute-start | bytes 73736
  423.9 26.4 %collective-permute-start.32 = (f32[16,384]{1,0:T(8,128)S(1)}, f32[16,384]{1,0:T(8,128)S(1)}, u32[]{:S(2)}, u32[]{:S(2)}) collective-permute-start(f32[16,384]{1,0:T(8,128)S(1)} %get-tuple-element.9), channel_id=1, source_target_pairs={{0,32},{8,40},{16,48},{24,56},{32,64},{40,72},{48,80},{56,88},{64,... | collective-permute-start | bytes 73736
  434.4 2.2 collective-permute-start.36
  436.7 16.6 %collective-permute-start.31 = (f32[16,384]{1,0:T(8,128)S(1)}, f32[16,384]{1,0:T(8,128)S(1)}, u32[]{:S(2)}, u32[]{:S(2)}) collective-permute-start(f32[16,384]{1,0:T(8,128)S(1)} %get-tuple-element.9), channel_id=1, source_target_pairs={{0,24},{8,32},{16,40},{24,48},{32,56},{40,64},{48,72},{56,80},{64,... | collective-permute-start | bytes 73736
  440.1 18.5 %collective-permute-start.30 = (f32[16,384]{1,0:T(8,128)S(1)}, f32[16,384]{1,0:T(8,128)S(1)}, u32[]{:S(2)}, u32[]{:S(2)}) collective-permute-start(f32[16,384]{1,0:T(8,128)S(1)} %get-tuple-element.9), channel_id=1, source_target_pairs={{0,16},{8,24},{16,32},{24,40},{32,48},{40,56},{48,64},{56,72},{64,... | collective-permute-start | bytes 73736
  444.1 18.1 %collective-permute-start.29 = (f32[16,384]{1,0:T(8,128)S(1)}, f32[16,384]{1,0:T(8,128)S(1)}, u32[]{:S(2)}, u32[]{:S(2)}) collective-permute-start(f32[16,384]{1,0:T(8,128)S(1)} %get-tuple-element.9), channel_id=1, source_target_pairs={{0,8},{8,16},{16,24},{24,32},{32,40},{40,48},{48,56},{56,64},{64,7... | collective-permute-start | bytes 73736
  446.0 21.5 %collective-permute-start.27 = (f32[16,384]{1,0:T(8,128)S(1)}, f32[16,384]{1,0:T(8,128)S(1)}, u32[]{:S(2)}, u32[]{:S(2)}) collective-permute-start(f32[16,384]{1,0:T(8,128)S(1)} %get-tuple-element.10), channel_id=1, source_target_pairs={{0,56},{8,64},{16,72},{24,80},{32,88},{40,96},{48,104},{56,112},{6... | collective-permute-start | bytes 73736
  450.4 18.4 %collective-permute-start.26 = (f32[16,384]{1,0:T(8,128)S(1)}, f32[16,384]{1,0:T(8,128)S(1)}, u32[]{:S(2)}, u32[]{:S(2)}) collective-permute-start(f32[16,384]{1,0:T(8,128)S(1)} %get-tuple-element.10), channel_id=1, source_target_pairs={{0,48},{8,56},{16,64},{24,72},{32,80},{40,88},{48,96},{56,104},{64... | collective-permute-start | bytes 73736
  453.3 20.9 %collective-permute-start.25 = (f32[16,384]{1,0:T(8,128)S(1)}, f32[16,384]{1,0:T(8,128)S(1)}, u32[]{:S(2)}, u32[]{:S(2)}) collective-permute-start(f32[16,384]{1,0:T(8,128)S(1)} %get-tuple-element.10), channel_id=1, source_target_pairs={{0,40},{8,48},{16,56},{24,64},{32,72},{40,80},{48,88},{56,96},{64,... | collective-permute-start | bytes 73736
  458.5 16.9 %collective-permute-start.24 = (f32[16,384]{1,0:T(8,128)S(1)}, f32[16,384]{1,0:T(8,128)S(1)}, u32[]{:S(2)}, u32[]{:S(2)}) collective-permute-start(f32[16,384]{1,0:T(8,128)S(1)} %get-tuple-element.10), channel_id=1, source_target_pairs={{0,32},{8,40},{16,48},{24,56},{32,64},{40,72},{48,80},{56,88},{64,... | collective-permute-start | bytes 73736
  462.2 15.9 %collective-permute-start.23 = (f32[16,384]{1,0:T(8,128)S(1)}, f32[16,384]{1,0:T(8,128)S(1)}, u32[]{:S(2)}, u32[]{:S(2)}) collective-permute-start(f32[16,384]{1,0:T(8,128)S(1)} %get-tuple-element.10), channel_id=1, source_target_pairs={{0,24},{8,32},{16,40},{24,48},{32,56},{40,64},{48,72},{56,80},{64,... | collective-permute-start | bytes 73736
  467.5 12.2 %collective-permute-start.22 = (f32[16,384]{1,0:T(8,128)S(1)}, f32[16,384]{1,0:T(8,128)S(1)}, u32[]{:S(2)}, u32[]{:S(2)}) collective-permute-start(f32[16,384]{1,0:T(8,128)S(1)} %get-tuple-element.10), channel_id=1, source_target_pairs={{0,16},{8,24},{16,32},{24,40},{32,48},{40,56},{48,64},{56,72},{64,... | collective-permute-start | bytes 73736
  468.8 13.8 %collective-permute-start.21 = (f32[16,384]{1,0:T(8,128)S(1)}, f32[16,384]{1,0:T(8,128)S(1)}, u32[]{:S(2)}, u32[]{:S(2)}) collective-permute-start(f32[16,384]{1,0:T(8,128)S(1)} %get-tuple-element.10), channel_id=1, source_target_pairs={{0,8},{8,16},{16,24},{24,32},{32,40},{40,48},{48,56},{56,64},{64,7... | collective-permute-start | bytes 73736
  474.2 13.9 %collective-permute-start.19 = (f32[16,384]{1,0:T(8,128)S(1)}, f32[16,384]{1,0:T(8,128)S(1)}, u32[]{:S(2)}, u32[]{:S(2)}) collective-permute-start(f32[16,384]{1,0:T(8,128)S(1)} %get-tuple-element.11), channel_id=1, source_target_pairs={{0,56},{8,64},{16,72},{24,80},{32,88},{40,96},{48,104},{56,112},{6... | collective-permute-start | bytes 73736
  475.5 14.9 %collective-permute-start.18 = (f32[16,384]{1,0:T(8,128)S(1)}, f32[16,384]{1,0:T(8,128)S(1)}, u32[]{:S(2)}, u32[]{:S(2)}) collective-permute-start(f32[16,384]{1,0:T(8,128)S(1)} %get-tuple-element.11), channel_id=1, source_target_pairs={{0,48},{8,56},{16,64},{24,72},{32,80},{40,88},{48,96},{56,104},{64... | collective-permute-start | bytes 73736
  478.0 14.4 %collective-permute-start.17 = (f32[16,384]{1,0:T(8,128)S(1)}, f32[16,384]{1,0:T(8,128)S(1)}, u32[]{:S(2)}, u32[]{:S(2)}) collective-permute-start(f32[16,384]{1,0:T(8,128)S(1)} %get-tuple-element.11), channel_id=1, source_target_pairs={{0,40},{8,48},{16,56},{24,64},{32,72},{40,80},{48,88},{56,96},{64,... | collective-permute-start | bytes 73736
  479.7 14.0 %collective-permute-start.16 = (f32[16,384]{1,0:T(8,128)S(1)}, f32[16,384]{1,0:T(8,128)S(1)}, u32[]{:S(2)}, u32[]{:S(2)}) collective-permute-start(f32[16,384]{1,0:T(8,128)S(1)} %get-tuple-element.11), channel_id=1, source_target_pairs={{0,32},{8,40},{16,48},{24,56},{32,64},{40,72},{48,80},{56,88},{64,... | collective-permute-start | bytes 73736
  482.6 12.5 %collective-permute-start.15 = (f32[16,384]{1,0:T(8,128)S(1)}, f32[16,384]{1,0:T(8,128)S(1)}, u32[]{:S(2)}, u32[]{:S(2)}) collective-permute-start(f32[16,384]{1,0:T(8,128)S(1)} %get-tuple-element.11), channel_id=1, source_target_pairs={{0,24},{8,32},{16,40},{24,48},{32,56},{40,64},{48,72},{56,80},{64,... | collective-permute-start | bytes 73736
  488.0 8.4 %collective-permute-start.14 = (f32[16,384]{1,0:T(8,128)S(1)}, f32[16,384]{1,0:T(8,128)S(1)}, u32[]{:S(2)}, u32[]{:S(2)}) collective-permute-start(f32[16,384]{1,0:T(8,128)S(1)} %get-tuple-element.11), channel_id=1, source_target_pairs={{0,16},{8,24},{16,32},{24,40},{32,48},{40,56},{48,64},{56,72},{64,... | collective-permute-start | bytes 73736
  490.4 7.3 %collective-permute-start.13 = (f32[16,384]{1,0:T(8,128)S(1)}, f32[16,384]{1,0:T(8,128)S(1)}, u32[]{:S(2)}, u32[]{:S(2)}) collective-permute-start(f32[16,384]{1,0:T(8,128)S(1)} %get-tuple-element.11), channel_id=1, source_target_pairs={{0,8},{8,16},{16,24},{24,32},{32,40},{40,48},{48,56},{56,64},{64,7... | collective-permute-start | bytes 73736
  492.5 13.4 %collective-permute-start.11 = (f32[16,384]{1,0:T(8,128)S(1)}, f32[16,384]{1,0:T(8,128)S(1)}, u32[]{:S(2)}, u32[]{:S(2)}) collective-permute-start(f32[16,384]{1,0:T(8,128)S(1)} %get-tuple-element.12), channel_id=1, source_target_pairs={{0,56},{8,64},{16,72},{24,80},{32,88},{40,96},{48,104},{56,112},{6... | collective-permute-start | bytes 73736
  493.8 14.3 %collective-permute-start.10 = (f32[16,384]{1,0:T(8,128)S(1)}, f32[16,384]{1,0:T(8,128)S(1)}, u32[]{:S(2)}, u32[]{:S(2)}) collective-permute-start(f32[16,384]{1,0:T(8,128)S(1)} %get-tuple-element.12), channel_id=1, source_target_pairs={{0,48},{8,56},{16,64},{24,72},{32,80},{40,88},{48,96},{56,104},{64... | collective-permute-start | bytes 73736
  495.1 6.9 %collective-permute-start.12 = (f32[12,384]{1,0:T(8,128)S(1)}, f32[12,384]{1,0:T(8,128)S(1)}, u32[]{:S(2)}, u32[]{:S(2)}) collective-permute-start(f32[12,384]{1,0:T(8,128)S(1)} %slice.30), channel_id=1, source_target_pairs={{0,64},{8,72},{16,80},{24,88},{32,96},{40,104},{48,112},{56,120},{... | collective-permute-start | bytes 55304
  496.4 14.2 %collective-permute-start.9 = (f32[16,384]{1,0:T(8,128)S(1)}, f32[16,384]{1,0:T(8,128)S(1)}, u32[]{:S(2)}, u32[]{:S(2)}) collective-permute-start(f32[16,384]{1,0:T(8,128)S(1)} %get-tuple-element.12), channel_id=1, source_target_pairs={{0,40},{8,48},{16,56},{24,64},{32,72},{40,80},{48,88},{56,96},{64,... | collective-permute-start | bytes 73736
  497.7 12.9 %collective-permute-start.8 = (f32[16,384]{1,0:T(8,128)S(1)}, f32[16,384]{1,0:T(8,128)S(1)}, u32[]{:S(2)}, u32[]{:S(2)}) collective-permute-start(f32[16,384]{1,0:T(8,128)S(1)} %get-tuple-element.12), channel_id=1, source_target_pairs={{0,32},{8,40},{16,48},{24,56},{32,64},{40,72},{48,80},{56,88},{64,... | collective-permute-start | bytes 73736
  502.0 8.6 %collective-permute-start.7 = (f32[16,384]{1,0:T(8,128)S(1)}, f32[16,384]{1,0:T(8,128)S(1)}, u32[]{:S(2)}, u32[]{:S(2)}) collective-permute-start(f32[16,384]{1,0:T(8,128)S(1)} %get-tuple-element.12), channel_id=1, source_target_pairs={{0,24},{8,32},{16,40},{24,48},{32,56},{40,64},{48,72},{56,80},{64,... | collective-permute-start | bytes 73736
  505.9 4.7 collective-permute-start.6
  508.1 3.4 collective-permute-start.5
where the time goes:
time: 514 us; the launch traced here: 513 us
  waiting for transfers between devices  247 us (48%)
  blocking collectives  103 us (20%)
  starting transfers between devices  97 us (19%)
  local copies, waits for them, and re-layouts  32.5 us (6%)
  other arithmetic  24.9 us (5%)
  matrix products  7.99 us (2%)
    ppermute x3, waiting for transfers between devices, passed_along(): lax.ppermute(array, axis, [(i, (i + by) % count) for i in range(count)])  213 us
    unnamed x1, blocking collectives  103 us
    unnamed x32, starting transfers between devices  92.3 us
    ppermute x1, waiting for transfers between devices, padded_2(): after = lax.ppermute(initial, axis, down)  31.3 us
    convert_element_type x1, other arithmetic, apply_current(): return (upper_plane - lower_plane).astype(jnp.bfloat16)  15.7 us
    unnamed x22, local copies, waits for them, and re-layouts  13.6 us
  transfers between devices with their start and end apart: 37, of which 6 were waited for; matrix products, arithmetic and copies ran while one was open for 5% of the time, Pallas kernels for 0%

commit v1 on v0

v1 whole, which is shorter than its diff:
```python
import jax
import jax.numpy as jnp
from jax import lax
from jax.experimental import pallas as pl
from jax.experimental.pallas import tpu as pltpu
from jax.sharding import PartitionSpec as P

PLANE = 2304
QUARTER = 576
CHUNK = 1152
SB = 384
PIECE = 128
BF16 = jnp.bfloat16
F32 = jnp.float32
SENT = jnp.float32
MESH = pl.DeviceIdType.MESH
NEIGHBOURS = (3, 1, 2)


def kernel(
    vec, perm, out,
    w, u, halo, it, vn, part, xrecv, xsum, zrecv, fin, finr,
    swap_s, swap_r, pair_s, pair_r, outer_s, outer_r, sib_s, sib_r,
    y1_s, y1_r, y2_s, y2_r, x_s, x_r, z_s, z_r, fin_s, fin_r,
):
    slab, blk = lax.axis_index("slab"), lax.axis_index("blk")
    x, zh, c = slab // 8, (slab // 2) % 4, slab % 2
    zl, y = blk // 4, blk % 4
    keeper = c == zl

    def dev(x_, zh_, c_, zl_, y_):
        return (x_ * 8 + zh_ * 2 + c_, zl_ * 4 + y_)

    def remote(src, dst, ss, rs, where):
        return pltpu.make_async_remote_copy(
            src_ref=src, dst_ref=dst, send_sem=ss, recv_sem=rs,
            device_id=where, device_id_type=MESH,
        )

    zz = (x * 4 + zh) * 2 + zl
    zo = lax.rem(zz + 32 + 2 * zl - 1, 32)
    outer_dev = dev(zo // 8, (zo // 2) % 4, c, zo % 2, y)
    up = dev(x, zh, c, zl, (y + 1) % 4)
    down = dev(x, zh, c, zl, (y + 3) % 4)
    sibling = dev(x, zh, 1 - c, zl, y)

    swaps = [remote(w.at[j], u.at[j], swap_s.at[j], swap_r.at[j], dev(x, zh, zl, c, y)) for j in range(3)]
    pairs = [
        remote(w.at[j, :, :, 1 - c], halo.at[c, j], pair_s.at[j], pair_r.at[j], dev(x, zh, zl, 1 - c, y))
        for j in range(3)
    ]
    outers = [
        remote(u.at[j, :, :, zl], halo.at[1 - zl, j], outer_s.at[j], outer_r.at[j], outer_dev)
        for j in range(3)
    ]
    hop1 = [
        [remote(u.at[j, d], vn.at[d, j], y1_s.at[d, j], y1_r.at[d, j], (up, down)[d]) for d in range(2)]
        for j in range(3)
    ]
    hu = (((y + 1) % 4) // 2, ((y + 3) % 4) // 2)
    hop2 = [
        [remote(vn.at[d, j, hu[d]], vn.at[2, j, d], y2_s.at[d, j], y2_r.at[d, j], (up, down)[d]) for d in range(2)]
        for j in range(3)
    ]

    with jax.named_scope("sort"):
        row = lax.broadcasted_iota(jnp.int32, (SB, SB), 0)
        onehot = jnp.where(row == perm[...], 1.0, 0.0).astype(BF16)

        def sort_chunk(i, carry):
            plane, q = i // 4, i % 4
            at = pl.multiple_of(i * QUARTER, QUARTER)
            got = jnp.dot(vec[pl.ds(at, QUARTER), :], onehot, preferred_element_type=F32).astype(BF16)
            for j in range(3):
                w[j, q % 2, q // 2, plane] = got[:, j * PIECE:(j + 1) * PIECE]

            @pl.when(keeper)
            def _():
                for j in range(3):
                    u[j, q % 2, q // 2, plane] = got[:, j * PIECE:(j + 1) * PIECE]

            return carry

        lax.fori_loop(0, 8, sort_chunk, 0)

    @pl.when(jnp.logical_not(keeper))
    def _():
        for j in range(3):
            swaps[j].start()
        for j in range(3):
            pairs[j].start()

    for j in range(3):
        @pl.when(jnp.logical_not(keeper))
        def _():
            swaps[j].wait_recv()

        for d in range(2):
            hop1[j][d].start()
        outers[j].start()
        if j > 0:
            for d in range(2):
                hop1[j - 1][d].wait_recv()
                hop2[j - 1][d].start()
    for d in range(2):
        hop1[2][d].wait_recv()
        hop2[2][d].start()

    @pl.when(keeper)
    def _():
        for j in range(3):
            pairs[j].start()

    for j in range(3):
        outers[j].wait_recv()
        pairs[j].wait_recv()

    with jax.named_scope("image"):
        def image_chunk(i, carry):
            par, half = i // 2, i % 2
            for j in range(3):
                mine = u[j, par, half].astype(F32)
                first = mine[1] - halo[0, j, par, half].astype(F32)
                second = halo[1, j, par, half].astype(F32) - mine[0]
                both = jnp.concatenate([first, second], axis=0)
                it[c, par, half, j * PIECE:(j + 1) * PIECE, :] = both.astype(BF16).T
            return carry

        lax.fori_loop(0, 4, image_chunk, 0)
    sib = remote(it.at[c], it.at[c], sib_s, sib_r, sibling)
    sib.start()

    xsend = [
        [
            remote(part.at[t, :, (x + d) % 4], xrecv.at[t, d - 1], x_s.at[t, d - 1], x_r.at[t, d - 1],
                   dev((x + d) % 4, zh, c, zl, y))
            for d in (1, 2, 3)
        ]
        for t in range(7)
    ]

    def wide(ref):
        return jnp.concatenate([ref(j).reshape(CHUNK, PIECE) for j in range(3)], axis=1)

    def put(t, value):
        part[t] = value.reshape(3, 4, 32, SB).astype(SENT)
        for copy in xsend[t]:
            copy.start()

    with jax.named_scope("diagonal"):
        def own_chunk(i, total):
            par, half = i // 2, i % 2
            return total + jnp.dot(
                it[c, par, half], wide(lambda j: u[j, par, half]), preferred_element_type=F32
            )

        put(0, lax.fori_loop(0, 4, own_chunk, jnp.zeros((SB, SB), F32)))

    sib.wait_recv()
    where = [(c, y)]
    for i, n in enumerate(NEIGHBOURS):
        wraps = jnp.where(y + n >= 4, 1, 0)
        same = wraps * c + (1 - wraps) * (1 - c)
        where.append((c, (y + n) % 4))
        if n == 2:
            for j in range(3):
                for d in range(2):
                    hop2[j][d].wait_recv()

        for kind in range(2):
            who = same if kind == 0 else 1 - same

            def chunk(s, total, i=i, n=n, who=who):
                par, half = (s, y // 2) if n == 2 else ((0, s) if n == 3 else (1, s))
                return total + jnp.dot(
                    it[who, par, half], wide(lambda j: vn[i, j, s]), preferred_element_type=F32
                )

            got = lax.fori_loop(0, 2, chunk, jnp.zeros((SB, SB), F32))
            put(1 + i + 3 * kind, got if kind == 0 else -got.T)
    for i, n in enumerate(NEIGHBOURS):
        wraps = jnp.where(y + n >= 4, 1, 0)
        same = wraps * c + (1 - wraps) * (1 - c)
        where.append((1 - same, y))

    slots = [0] + [4 - n for n in NEIGHBOURS] + [3 + n for n in NEIGHBOURS]
    z8 = zh * 2 + zl
    for t in range(7):
        for copy in xsend[t]:
            copy.wait_recv()
        total = part[t, :, x].astype(F32)
        for d in range(3):
            total = total + xrecv[t, d].astype(F32)
        xsum[t] = total
        zp, yp = where[t]
        here = (zp == zl) & (yp == y) & keeper
        for h in range(4):
            is_self = here & (zh == h)

            @pl.when(is_self)
            def _():
                zrecv[slots[t], z8] = total[:, 8 * h:8 * h + 8]

            @pl.when(jnp.logical_not(is_self))
            def _():
                remote(xsum.at[t, :, 8 * h:8 * h + 8], zrecv.at[slots[t], z8], z_s.at[t], z_r.at[slots[t]],
                       dev(x, h, zp, zp, yp)).start()

    last = remote(fin, finr, fin_s, fin_r, sibling)

    def write(ref):
        for k in range(4):
            for j in range(3):
                rows = ref[k, j]
                out[k, 4 * j:4 * j + 4, :] = jnp.where(c == 0, rows[0:4], rows[4:8])

    @pl.when(keeper)
    def _():
        for s in range(7):
            if s == 0:
                few = y < 4
            elif s < 4:
                few = y > 4
            else:
                few = y + (s - 3) < 4

            @pl.when(few)
            def _():
                pltpu.make_async_copy(zrecv.at[s, 0:7], zrecv.at[s, 0:7], z_r.at[s]).wait()

            @pl.when(jnp.logical_not(few))
            def _():
                pltpu.make_async_copy(zrecv.at[s], zrecv.at[s], z_r.at[s]).wait()

        src = lax.broadcasted_iota(jnp.int32, (SB, SB), 0)
        dst = lax.broadcasted_iota(jnp.int32, (SB, SB), 1)
        slot = ((src % PIECE) // 4) * 12 + (src // PIECE) * 4 + src % 4
        unsort = jnp.where(slot == dst, 1.0, 0.0).astype(F32)
        for k in range(4):
            total = jnp.sum(zrecv[k], axis=0)
            if k > 0:
                total = total + jnp.sum(zrecv[3 + k], axis=0)
            flat = jnp.dot(total.reshape(24, SB), unsort, precision=lax.Precision.HIGHEST,
                           preferred_element_type=F32)
            fin[k] = flat.reshape(3, 8, SB)
        last.start()
        write(fin)
        last.wait_send()

    @pl.when(jnp.logical_not(keeper))
    def _():
        last.wait_recv()
        write(finr)
        for j in range(3):
            swaps[j].wait_send()

    for j in range(3):
        pairs[j].wait_send()
        outers[j].wait_send()
        for d in range(2):
            hop1[j][d].wait_send()
            hop2[j][d].wait_send()
    sib.wait_send()
    for t in range(7):
        for copy in xsend[t]:
            copy.wait_send()
        zp, yp = where[t]
        here = (zp == zl) & (yp == y) & keeper

        @pl.when(here)
        def _():
            pltpu.make_async_copy(xsum.at[t, :, 0:24], xsum.at[t, :, 0:24], z_s.at[t]).wait()

        @pl.when(jnp.logical_not(here))
        def _():
            pltpu.make_async_copy(xsum.at[t], xsum.at[t], z_s.at[t]).wait()


def on_device(vectors, state_order):
    perm = state_order.reshape(32, 3, 4).transpose(1, 0, 2).reshape(1, SB)
    dma = pltpu.SemaphoreType.DMA
    return pl.pallas_call(
        kernel,
        out_shape=jax.ShapeDtypeStruct((4, 12, SB), F32),
        in_specs=[pl.BlockSpec(memory_space=pltpu.VMEM)] * 2,
        out_specs=pl.BlockSpec(memory_space=pltpu.VMEM),
        scratch_shapes=[
            pltpu.VMEM((3, 2, 2, 2, QUARTER, PIECE), BF16),
            pltpu.VMEM((3, 2, 2, 2, QUARTER, PIECE), BF16),
            pltpu.VMEM((2, 3, 2, 2, QUARTER, PIECE), BF16),
            pltpu.VMEM((2, 2, 2, SB, CHUNK), BF16),
            pltpu.VMEM((3, 3, 2, 2, QUARTER, PIECE), BF16),
            pltpu.VMEM((7, 3, 4, 32, SB), SENT),
            pltpu.VMEM((7, 3, 3, 32, SB), SENT),
            pltpu.VMEM((7, 3, 32, SB), F32),
            pltpu.VMEM((7, 8, 3, 8, SB), F32),
            pltpu.VMEM((4, 3, 8, SB), F32),
            pltpu.VMEM((4, 3, 8, SB), F32),
            dma((3,)), dma((3,)), dma((3,)), dma((3,)), dma((3,)), dma((3,)),
            dma, dma,
            dma((2, 3)), dma((2, 3)), dma((2, 3)), dma((2, 3)),
            dma((7, 3)), dma((7, 3)), dma((7,)), dma((7,)),
            dma, dma,
        ],
        compiler_params=pltpu.CompilerParams(
            has_side_effects=True, vmem_limit_bytes=60 * 1024 * 1024
        ),
        cost_estimate=pl.CostEstimate(flops=6_000_000_000, bytes_accessed=4_000_000, transcendentals=0),
    )(vectors, perm)


def solution(mesh):
    return jax.shard_map(
        on_device,
        mesh=mesh,
        in_specs=(P("slab", "blk"), P("blk")),
        out_specs=P(None, "slab", "blk"),
        check_vma=False,
    )
```

time: 514 us -> 146 us (0.28)
  waiting for transfers between devices: 247 us -> 0 us
  Pallas kernels: 0 us -> 143 us
  blocking collectives: 103 us -> 0 us
  starting transfers between devices: 97 us -> 0 us
  local copies, waits for them, and re-layouts: 32.5 us -> 3.03 us
  other arithmetic: 24.9 us -> 0 us
  matrix products: 7.99 us -> 0 us
    ppermute x5 -> x0, waiting for transfers between devices: 245 us -> none  [the longest x3 213 us: passed_along(): lax.ppermute(array, axis, [(i, (i + by) % count) for i in range(count)])]
    pallas_call x0 -> x1, Pallas kernels: none -> 143 us  [on_device(): pl.pallas_call(kernel, out_shape=jax.ShapeDtypeStruct((4, 12, SB), F32),...]
    unnamed x1 -> x0, blocking collectives: 103 us -> none
    unnamed x32 -> x0, starting transfers between devices: 92.3 us -> none
    convert_element_type x1 -> x0, other arithmetic: 15.7 us -> none  [apply_current(): return (upper_plane - lower_plane).astype(jnp.bfloat16)]
    unnamed x22 -> x0, local copies, waits for them, and re-layouts: 13.6 us -> none
    select_n x3 -> x0, other arithmetic: 8.44 us -> none  [on_device(): sorted_vec = jnp.take(vectors, state_order, axis=1)]
    ppermute x2 -> x0, local copies, waits for them, and re-layouts: 8.41 us -> none  [the longest x1 4.21 us: padded_2(): before = lax.ppermute(last, axis, up)]
  transfers between devices with their start and end apart: 37 -> 0, of which waited for: 6 -> 0; matrix products, arithmetic and copies ran while one was open for 5% -> 0% of each run, Pallas kernels for 0% -> 0%
where the time goes in v1:
time: 146 us
  Pallas kernels  143 us (98%)
  local copies, waits for them, and re-layouts  3.03 us (2%)
    pallas_call x1, Pallas kernels, on_device(): pl.pallas_call(kernel, out_shape=jax.ShapeDtypeStruct((4, 12, SB), F32),...  143 us

profile of v1, /device:TPU:1, one launch (start us, length us, event | category | flops | bytes accessed | tf_op | source)
XLA Modules:
  0.0 145.9 jit_solution(14623519763314140533)
XLA Ops:
  0.0 0.8 reshape.6
  0.8 0.7 reshape.7.perm
  1.5 142.8 %shard_map.28 = f32[4,12,384]{2,1,0:T(8,128)} custom-call(bf16[4608,384]{1,0:T(8,128)(2,1)} %vec.1, s32[1,384]{1,0:T(1,128)} %reshape.7.perm), custom_call_target="tpu_custom_call" | custom-call | flops 6000000000 | bytes 4000000 | tf_op jit(solution)/shard_map/pallas_call | solution.py:282
  144.3 1.6 %copy.5 = f32[4,12,384]{2,0,1:T(4,128)} copy(f32[4,12,384]{2,1,0:T(8,128)} %shard_map.28) | data formatting | bytes 147456 | tf_op jit(solution)/shard_map/pallas_call | solution.py:282
  (1 shorter events, 0.0 us)

commit v2 on v1

--- a/solution.py
+++ b/solution.py
@@ -12,16 +12,16 @@
 PIECE = 128
 BF16 = jnp.bfloat16
 F32 = jnp.float32
-SENT = jnp.float32
+SENT = jnp.bfloat16
 MESH = pl.DeviceIdType.MESH
 NEIGHBOURS = (3, 1, 2)
 
 
 def kernel(
-    vec, perm, out,
-    w, u, halo, it, vn, part, xrecv, xsum, zrecv, fin, finr,
+    vec_hbm, order, out,
+    vec, w, u, halo, it, vn, part, xrecv, xsum, zrecv, fin, finr,
     swap_s, swap_r, pair_s, pair_r, outer_s, outer_r, sib_s, sib_r,
-    y1_s, y1_r, y2_s, y2_r, x_s, x_r, z_s, z_r, fin_s, fin_r,
+    y1_s, y1_r, y2_s, y2_r, x_s, x_r, z_s, z_r, fin_s, fin_r, load,
 ):
     slab, blk = lax.axis_index("slab"), lax.axis_index("blk")
     x, zh, c = slab // 8, (slab // 2) % 4, slab % 2
@@ -44,6 +44,25 @@
     down = dev(x, zh, c, zl, (y + 3) % 4)
     sibling = dev(x, zh, 1 - c, zl, y)
 
+    fetch = pltpu.make_async_copy(vec_hbm, vec, load)
+    fetch.start()
+    barrier = pltpu.get_barrier_semaphore()
+
+    def greet(where):
+        pl.semaphore_signal(barrier, inc=1, device_id=where, device_id_type=MESH)
+
+    me = blk * 8 + zh * 2 + c
+
+    def greet_plane(i, carry):
+        other = lax.rem(me + 1 + i, 64)
+        greet((x * 8 + other % 8, other // 8))
+        return carry
+
+    lax.fori_loop(0, 63, greet_plane, 0)
+    for d in (1, 2, 3):
+        greet(dev((x + d) % 4, zh, c, zl, y))
+    greet(outer_dev)
+
     swaps = [remote(w.at[j], u.at[j], swap_s.at[j], swap_r.at[j], dev(x, zh, zl, c, y)) for j in range(3)]
     pairs = [
         remote(w.at[j, :, :, 1 - c], halo.at[c, j], pair_s.at[j], pair_r.at[j], dev(x, zh, zl, 1 - c, y))
@@ -65,7 +84,13 @@
 
     with jax.named_scope("sort"):
         row = lax.broadcasted_iota(jnp.int32, (SB, SB), 0)
-        onehot = jnp.where(row == perm[...], 1.0, 0.0).astype(BF16)
+        picked = jnp.where(row == order[...][None, :], 1.0, 0.0).astype(BF16)
+        src = lax.broadcasted_iota(jnp.int32, (SB, SB), 0)
+        dst = lax.broadcasted_iota(jnp.int32, (SB, SB), 1)
+        slot = ((dst % PIECE) // 4) * 12 + (dst // PIECE) * 4 + dst % 4
+        laid = jnp.where(slot == src, 1.0, 0.0).astype(BF16)
+        onehot = jnp.dot(picked, laid, preferred_element_type=F32).astype(BF16)
+        fetch.wait()
 
         def sort_chunk(i, carry):
             plane, q = i // 4, i % 4
@@ -82,6 +107,7 @@
             return carry
 
         lax.fori_loop(0, 8, sort_chunk, 0)
+    pl.semaphore_wait(barrier, 67)
 
     @pl.when(jnp.logical_not(keeper))
     def _():
@@ -277,14 +303,14 @@
 
 
 def on_device(vectors, state_order):
-    perm = state_order.reshape(32, 3, 4).transpose(1, 0, 2).reshape(1, SB)
     dma = pltpu.SemaphoreType.DMA
     return pl.pallas_call(
         kernel,
         out_shape=jax.ShapeDtypeStruct((4, 12, SB), F32),
-        in_specs=[pl.BlockSpec(memory_space=pltpu.VMEM)] * 2,
+        in_specs=[pl.BlockSpec(memory_space=pl.ANY), pl.BlockSpec(memory_space=pltpu.VMEM)],
         out_specs=pl.BlockSpec(memory_space=pltpu.VMEM),
         scratch_shapes=[
+            pltpu.VMEM((2 * PLANE, SB), BF16),
             pltpu.VMEM((3, 2, 2, 2, QUARTER, PIECE), BF16),
             pltpu.VMEM((3, 2, 2, 2, QUARTER, PIECE), BF16),
             pltpu.VMEM((2, 3, 2, 2, QUARTER, PIECE), BF16),
@@ -300,13 +326,13 @@
             dma, dma,
             dma((2, 3)), dma((2, 3)), dma((2, 3)), dma((2, 3)),
             dma((7, 3)), dma((7, 3)), dma((7,)), dma((7,)),
-            dma, dma,
+            dma, dma, dma,
         ],
         compiler_params=pltpu.CompilerParams(
-            has_side_effects=True, vmem_limit_bytes=60 * 1024 * 1024
+            collective_id=0, has_side_effects=True, vmem_limit_bytes=60 * 1024 * 1024
         ),
         cost_estimate=pl.CostEstimate(flops=6_000_000_000, bytes_accessed=4_000_000, transcendentals=0),
-    )(vectors, perm)
+    )(vectors, state_order)
 
 
 def solution(mesh):

time: 146 us -> 117 us (0.80)
  Pallas kernels: 143 us -> 116 us
  local copies, waits for them, and re-layouts: 3.03 us -> 1.56 us
    pallas_call x1, Pallas kernels: 143 us -> 116 us  [on_device(): pl.pallas_call(kernel, out_shape=jax.ShapeDtypeStruct((4, 12, SB), F32),...]
    reshape x2 -> x0, local copies, waits for them, and re-layouts: 1.47 us -> none  [on_device(): perm = state_order.reshape(32, 3, 4).transpose(1, 0, 2).reshape(1, SB)]
where the time goes in v2:
time: 117 us
  Pallas kernels  116 us (99%)
  local copies, waits for them, and re-layouts  1.56 us (1%)
    pallas_call x1, Pallas kernels, on_device(): pl.pallas_call(kernel, out_shape=jax.ShapeDtypeStruct((4, 12, SB), F32),...  116 us

profile of v2, /device:TPU:1, one launch (start us, length us, event | category | flops | bytes accessed | tf_op | source)
XLA Modules:
  0.0 117.2 jit_solution(3923493313809904026)
XLA Ops:
  0.0 115.7 %shard_map.28 = f32[4,12,384]{2,1,0:T(8,128)} custom-call(bf16[4608,384]{1,0:T(8,128)(2,1)} %vec_hbm.1, s32[384]{0:T(512)} %order.1), custom_call_target="tpu_custom_call" | custom-call | flops 6000000000 | bytes 4000000 | tf_op jit(solution)/shard_map/pallas_call | solution.py:307
  115.7 1.6 %copy.3 = f32[4,12,384]{2,0,1:T(4,128)} copy(f32[4,12,384]{2,1,0:T(8,128)} %shard_map.28) | data formatting | bytes 147456 | tf_op jit(solution)/shard_map/pallas_call | solution.py:307

commit v3 on v2

v3 whole, which is shorter than its diff:
```python
import jax
import jax.numpy as jnp
from jax import lax
from jax.experimental import pallas as pl
from jax.experimental.pallas import tpu as pltpu
from jax.sharding import PartitionSpec as P

PLANE = 2304
QUARTER = 576
CHUNK = 1152
SB = 384
PIECE = 128
BF16 = jnp.bfloat16
F32 = jnp.float32
SENT = jnp.bfloat16
MESH = pl.DeviceIdType.MESH
NEIGHBOURS = (3, 1, 2)
TILE = {(2, 0): 2, (2, 1): 3, (0, 0): 4, (0, 1): 5, (1, 0): 6, (1, 1): 7, (0, 2): 8, (1, 2): 9}


def kernel(
    vec_hbm, order, out,
    vec, w, u, halo, it, vn, whole, part, xrecv, zsend, zrecv, fin, finr,
    swap_s, swap_r, pair_s, pair_r, outer_s, outer_r, sib_s, sib_r,
    y1_s, y1_r, y2_s, y2_r, x_s, x_r, z_s, z_r, fin_s, fin_r, load, sent,
):
    slab, blk = lax.axis_index("slab"), lax.axis_index("blk")
    x, zh, c = slab // 8, (slab // 2) % 4, slab % 2
    zl, y = blk // 4, blk % 4
    keeper = c == zl

    def dev(x_, zh_, c_, zl_, y_):
        return (x_ * 8 + zh_ * 2 + c_, zl_ * 4 + y_)

    def remote(src, dst, ss, rs, where):
        return pltpu.make_async_remote_copy(
            src_ref=src, dst_ref=dst, send_sem=ss, recv_sem=rs,
            device_id=where, device_id_type=MESH,
        )

    zz = (x * 4 + zh) * 2 + zl
    zo = lax.rem(zz + 32 + 2 * zl - 1, 32)
    outer_dev = dev(zo // 8, (zo // 2) % 4, c, zo % 2, y)
    up = dev(x, zh, c, zl, (y + 1) % 4)
    down = dev(x, zh, c, zl, (y + 3) % 4)
    sibling = dev(x, zh, 1 - c, zl, y)

    fetch = pltpu.make_async_copy(vec_hbm, vec, load)
    fetch.start()
    zrecv[:, :, 0:16] = jnp.zeros((7, 8, 16, PIECE), SENT)
    zrecv[:, :, 80:96] = jnp.zeros((7, 8, 16, PIECE), SENT)
    barrier = pltpu.get_barrier_semaphore()

    def greet(where):
        pl.semaphore_signal(barrier, inc=1, device_id=where, device_id_type=MESH)

    @pl.when(keeper)
    def _():
        me = zh * 8 + zl * 4 + y

        def greet_source(i, carry):
            other = lax.rem(me + 1 + i, 32)
            greet(dev(x, other // 8, c, (other // 4) % 2, other % 4))
            return carry

        def greet_crossing(i, carry):
            greet(dev(x, i // 2, 1 - c, i % 2, y))
            return carry

        lax.fori_loop(0, 31, greet_source, 0)
        lax.fori_loop(0, 8, greet_crossing, 0)

    @pl.when(jnp.logical_not(keeper))
    def _():
        def greet_owner(i, carry):
            greet(dev(x, i // 4, c, c, i % 4))
            return carry

        def greet_crossing(i, carry):
            greet(dev(x, i, 1 - c, 1 - c, y))
            return carry

        lax.fori_loop(0, 16, greet_owner, 0)
        lax.fori_loop(0, 4, greet_crossing, 0)
        greet(dev(x, zh, 1 - c, 1 - zl, y))
        greet(up)
        greet(down)

    for d in (1, 2, 3):
        greet(dev((x + d) % 4, zh, c, zl, y))
    greet(outer_dev)

    swap_dev = dev(x, zh, zl, c, y)
    swaps = [remote(w.at[j], u.at[j], swap_s.at[j], swap_r.at[j], swap_dev) for j in range(3)]
    pairs = [
        remote(w.at[j, :, :, 1 - c], halo.at[c, j], pair_s.at[j], pair_r.at[j], dev(x, zh, zl, 1 - c, y))
        for j in range(3)
    ]
    outers = [
        remote(u.at[j, :, :, zl], halo.at[1 - zl, j], outer_s.at[j], outer_r.at[j], outer_dev)
        for j in range(3)
    ]
    hop1 = [
        [remote(u.at[j, d], vn.at[d, j], y1_s.at[d, j], y1_r.at[d, j], (up, down)[d]) for d in range(2)]
        for j in range(3)
    ]
    hu = (((y + 1) % 4) // 2, ((y + 3) % 4) // 2)
    hop2 = [
        [remote(vn.at[d, j, hu[d]], vn.at[2, j, d], y2_s.at[d, j], y2_r.at[d, j], (up, down)[d]) for d in range(2)]
        for j in range(3)
    ]
    sib = [remote(it.at[c, j], it.at[c, j], sib_s.at[j], sib_r.at[j], sibling) for j in range(3)]

    def go(copies):
        for copy in copies:
            copy.start()

    def arrive(copies):
        for copy in copies:
            copy.wait_recv()

    with jax.named_scope("sort"):
        row = lax.broadcasted_iota(jnp.int32, (SB, SB), 0)
        picked = jnp.where(row == order[...][None, :], 1.0, 0.0).astype(BF16)
        src = lax.broadcasted_iota(jnp.int32, (SB, SB), 0)
        dst = lax.broadcasted_iota(jnp.int32, (SB, SB), 1)
        slot = ((dst % PIECE) // 4) * 12 + (dst // PIECE) * 4 + dst % 4
        laid = jnp.where(slot == src, 1.0, 0.0).astype(BF16)
        onehot = jnp.dot(picked, laid, preferred_element_type=F32).astype(BF16)
        fetch.wait()

        def sort_chunk(i, carry):
            plane, q = i // 4, i % 4
            at = pl.multiple_of(i * QUARTER, QUARTER)
            got = jnp.dot(vec[pl.ds(at, QUARTER), :], onehot, preferred_element_type=F32).astype(BF16)
            for j in range(3):
                w[j, q % 2, q // 2, plane] = got[:, j * PIECE:(j + 1) * PIECE]

            @pl.when(keeper)
            def _():
                for j in range(3):
                    u[j, q % 2, q // 2, plane] = got[:, j * PIECE:(j + 1) * PIECE]

            return carry

        lax.fori_loop(0, 8, sort_chunk, 0)
    pl.semaphore_wait(barrier, jnp.where(keeper, 43, 27))

    def image(lo, hi):
        def image_chunk(i, carry):
            par, half = i // 2, i % 2
            for j in range(lo, hi):
                mine = u[j, par, half].astype(F32)
                below = mine[1] - halo[0, j, par, half].astype(F32)
                above = halo[1, j, par, half].astype(F32) - mine[0]
                both = jnp.concatenate([below, above], axis=0)
                it[c, j, par, half] = both.astype(BF16).T
            return carry

        lax.fori_loop(0, 4, image_chunk, 0)

    def wide(pieces):
        return jnp.concatenate([piece.reshape(CHUNK, PIECE) for piece in pieces], axis=1)

    def product(n, who, rows, cols):
        def chunk(s, total):
            if n == 0:
                par, half = s // 2, s % 2
                right = wide([u[j, par, half] for j in cols])
            else:
                par, half = {1: (1, s), 2: (s, y // 2), 3: (0, s)}[n]
                right = wide([vn[NEIGHBOURS.index(n), j, s] for j in cols])
            left = jnp.concatenate([it[who, i, par, half] for i in rows], axis=0)
            return total + jnp.dot(left, right, preferred_element_type=F32)

        zero = jnp.zeros((PIECE * len(rows), PIECE * len(cols)), F32)
        return lax.fori_loop(0, 4 if n == 0 else 2, chunk, zero)

    def kind(t):
        if t == 0:
            return True, c, y, 0
        n, own = (t - 1) % 3 + 1, t < 4
        wraps = y + n >= 4
        matched = wraps if own else jnp.logical_not(wraps)
        zp = jnp.where(matched, c, c if own else 1 - c)
        yp = jnp.where(matched, (y + n) % 4, y)
        return matched, zp, yp, jnp.where(matched, 4 - n, 3 + n)

    def put(t, rows, cols, last):
        n = 0 if t == 0 else (t - 1) % 3 + 1
        got = product(n, c if t < 4 else 1 - c, rows, cols)
        matched = kind(t)[0]

        def tiles(swapped):
            for a, i in enumerate(rows):
                for b, j in enumerate(cols):
                    tile = got[a * PIECE:(a + 1) * PIECE, b * PIECE:(b + 1) * PIECE]
                    at = (j, i) if swapped else (i, j)
                    tile = -tile.T if swapped else tile
                    slot = last[int(swapped)] if at == (2, 2) else TILE[at]
                    whole[t, slot] = tile.reshape(4, 32, PIECE)
                    part[t, slot] = tile.reshape(4, 32, PIECE).astype(SENT)

        if t == 0:
            tiles(False)
            return
        pl.when(matched)(lambda: tiles(False))
        pl.when(jnp.logical_not(matched))(lambda: tiles(True))

    def xcopies(t, phase, start, length):
        run = pl.ds(start, length)
        return [
            remote(part.at[t, run, (x + d) % 4], xrecv.at[t, d - 1, run], x_s.at[t, phase, d - 1],
                   x_r.at[t, phase, d - 1], dev((x + d) % 4, zh, c, zl, y))
            for d in (1, 2, 3)
        ]

    z8 = zh * 2 + zl

    def collect(t, phase, start, length):
        arrive(xcopies(t, phase, start, length))
        run = pl.ds(start, length)
        total = whole[t, run, x]
        for d in range(3):
            total = total + xrecv[t, d, run].astype(F32)
        total = total.astype(SENT)
        rows = pl.ds(pl.multiple_of(8 * start, 16), 8 * length)
        _, zp, yp, slot = kind(t)
        here = (zp == zl) & (yp == y) & keeper
        for h in range(4):
            is_self = here & (zh == h)
            share = total[:, 8 * h:8 * h + 8].reshape(8 * length, PIECE)

            @pl.when(is_self)
            def _():
                zrecv[slot, z8, rows] = share

            @pl.when(jnp.logical_not(is_self))
            def _():
                zsend[t, h, rows] = share
                remote(zsend.at[t, h, rows], zrecv.at[slot, z8, rows], z_s.at[t], z_r.at[slot],
                       dev(x, h, zp, zp, yp)).start()

    def side(t, one, other):
        return jnp.where(kind(t)[0], one, other)

    def settle(copies):
        for copy in copies:
            copy.wait_send()

    def done(runs):
        for j in range(3):
            settle([outers[j], sib[j]] + hop1[j] + hop2[j])
        for run in runs:
            settle(xcopies(*run))
        for t in range(7):
            _, zp, yp, _ = kind(t)
            here = (zp == zl) & (yp == y) & keeper

            @pl.when(here)
            def _():
                pltpu.make_async_copy(zsend.at[t, 0:3, 0:80], zsend.at[t, 0:3, 0:80], z_s.at[t]).wait()

            @pl.when(jnp.logical_not(here))
            def _():
                pltpu.make_async_copy(zsend.at[t, :, 0:80], zsend.at[t, :, 0:80], z_s.at[t]).wait()

    final = remote(fin, finr, fin_s, fin_r, sibling)

    def write(ref):
        for k in range(4):
            for j in range(3):
                rows = ref[k, j]
                out[k, 4 * j:4 * j + 4, :] = jnp.where(c == 0, rows[0:4], rows[4:8])

    def keep():
        everything = (0, 1, 2)
        pairs[0].start()
        for j in range(3):
            go(hop1[j])
        go(outers)
        pairs[0].wait_send()
        pl.semaphore_signal(sent, inc=1, device_id=sibling, device_id_type=MESH)
        for j in range(3):
            arrive(hop1[j])
            go(hop2[j])

        def ready(j):
            arrive([pairs[j], outers[j]])
            image(j, j + 1)
            sib[j].start()

        ready(0)
        for j in range(3):
            arrive(hop2[j])
        pl.semaphore_wait(sent, 1)
        pairs[1].start()
        ready(1)
        runs = [(t, 0, side(t, 4, 2), 6) for t in range(7)]
        rest = [(t, 1, side(t, 0, 8), 4) for t in range(7)]

        def early(t):
            put(t, (0, 1), everything, (0, 0))
            go(xcopies(*runs[t]))

        def late(t):
            put(t, (2,), everything, (0, 10))
            go(xcopies(*rest[t]))

        for t in range(4):
            early(t)
        pairs[1].wait_send()
        pairs[2].start()
        ready(2)
        for t in range(4):
            late(t)
        for t in range(4):
            collect(*runs[t])
        arrive(sib[:2])
        for t in (4, 5, 6):
            early(t)
        for t in range(4):
            collect(*rest[t])
        arrive(sib[2:])
        for t in (4, 5, 6):
            late(t)
        for t in (4, 5, 6):
            collect(*runs[t])
        for t in (4, 5, 6):
            collect(*rest[t])

        for s in range(7):
            if s == 0:
                few = y < 4
            elif s < 4:
                few = y > 4
            else:
                few = y + (s - 3) < 4

            @pl.when(few)
            def _():
                pltpu.make_async_copy(zrecv.at[s, 0:7, 0:80], zrecv.at[s, 0:7, 0:80], z_r.at[s]).wait()

            @pl.when(jnp.logical_not(few))
            def _():
                pltpu.make_async_copy(zrecv.at[s, :, 0:80], zrecv.at[s, :, 0:80], z_r.at[s]).wait()

        src = lax.broadcasted_iota(jnp.int32, (SB, SB), 0)
        dst = lax.broadcasted_iota(jnp.int32, (SB, SB), 1)
        unsort = jnp.where(((src % PIECE) // 4) * 12 + (src // PIECE) * 4 + src % 4 == dst, 1.0, 0.0).astype(F32)
        for k in range(4):
            total = jnp.sum(zrecv[k].astype(F32), axis=0)
            if k > 0:
                total = total + jnp.sum(zrecv[3 + k].astype(F32), axis=0)
            at = [total[8 * i:8 * i + 8] for i in range(12)]
            flat = jnp.concatenate([
                jnp.concatenate([at[4], at[5], at[8]], axis=1),
                jnp.concatenate([at[6], at[7], at[9]], axis=1),
                jnp.concatenate([at[2], at[3], at[0] + at[10]], axis=1),
            ], axis=0)
            flat = jnp.dot(flat, unsort, precision=lax.Precision.HIGHEST, preferred_element_type=F32)
            fin[k] = flat.reshape(3, 8, SB)
        final.start()
        write(fin)
        final.wait_send()
        pairs[2].wait_send()
        done(runs + rest)

    def swap():
        everything = (0, 1, 2)
        def ready(j):
            arrive([pairs[j], outers[j]])
            image(j, j + 1)
            sib[j].start()

        go(pairs)
        swaps[0].start()
        pl.semaphore_wait(sent, 1)
        swaps[1].start()
        swaps[0].wait_send()
        swaps[2].start()
        swaps[0].wait_recv()
        go(hop1[0])
        outers[0].start()
        ready(0)
        swaps[1].wait_send()
        swaps[1].wait_recv()
        go(hop1[1])
        outers[1].start()
        arrive(hop1[0])
        go(hop2[0])
        swaps[2].wait_send()
        pl.semaphore_signal(sent, inc=1, device_id=sibling, device_id_type=MESH)
        swaps[2].wait_recv()
        go(hop1[2])
        outers[2].start()
        arrive(hop1[1])
        go(hop2[1])
        arrive(hop2[0])
        arrive(hop2[1])
        arrive(sib)
        runs = [(t, 0, 4, 4) for t in range(4)] + [(t, 0, side(t, 2, 4), 6) for t in (4, 5, 6)]
        for t in (4, 5, 6):
            put(t, everything, (0, 1), (0, 0))
            go(xcopies(*runs[t]))
        arrive(hop1[2])
        go(hop2[2])
        ready(1)
        for t in range(4):
            put(t, (0, 1), (0, 1), (0, 0))
            go(xcopies(*runs[t]))
        for t in (4, 5, 6):
            collect(*runs[t])
        arrive(hop2[2])
        rest = []
        for t in (4, 5, 6):
            put(t, everything, (2,), (10, 0))
            rest.append((t, 1, side(t, 8, 0), 4))
            go(xcopies(*rest[-1]))
        ready(2)
        for t in range(4):
            put(t, (2,), everything, (0, 0))
            put(t, (0, 1), (2,), (0, 0))
            rest += [(t, 1, 0, 4), (t, 2, 8, 2)]
            go(xcopies(*rest[-2]))
            go(xcopies(*rest[-1]))
        for t in range(4):
            collect(*runs[t])
        for run in rest:
            collect(*run)
        settle(pairs)
        done(runs + rest)
        final.wait_recv()
        write(finr)

    pl.when(keeper)(keep)
    pl.when(jnp.logical_not(keeper))(swap)


def on_device(vectors, state_order):
    dma = pltpu.SemaphoreType.DMA
    return pl.pallas_call(
        kernel,
        out_shape=jax.ShapeDtypeStruct((4, 12, SB), F32),
        in_specs=[pl.BlockSpec(memory_space=pl.ANY), pl.BlockSpec(memory_space=pltpu.VMEM)],
        out_specs=pl.BlockSpec(memory_space=pltpu.VMEM),
        scratch_shapes=[
            pltpu.VMEM((2 * PLANE, SB), BF16),
            pltpu.VMEM((3, 2, 2, 2, QUARTER, PIECE), BF16),
            pltpu.VMEM((3, 2, 2, 2, QUARTER, PIECE), BF16),
            pltpu.VMEM((2, 3, 2, 2, QUARTER, PIECE), BF16),
            pltpu.VMEM((2, 3, 2, 2, PIECE, CHUNK), BF16),
            pltpu.VMEM((3, 3, 2, 2, QUARTER, PIECE), BF16),
            pltpu.VMEM((7, 12, 4, 32, PIECE), F32),
            pltpu.VMEM((7, 12, 4, 32, PIECE), SENT),
            pltpu.VMEM((7, 3, 12, 32, PIECE), SENT),
            pltpu.VMEM((7, 4, 96, PIECE), SENT),
            pltpu.VMEM((7, 8, 96, PIECE), SENT),
            pltpu.VMEM((4, 3, 8, SB), F32),
            pltpu.VMEM((4, 3, 8, SB), F32),
            dma((3,)), dma((3,)), dma((3,)), dma((3,)), dma((3,)), dma((3,)),
            dma((3,)), dma((3,)),
            dma((2, 3)), dma((2, 3)), dma((2, 3)), dma((2, 3)),
            dma((7, 3, 3)), dma((7, 3, 3)), dma((7,)), dma((7,)),
            dma, dma, dma, pltpu.SemaphoreType.REGULAR,
        ],
        compiler_params=pltpu.CompilerParams(
            collective_id=0, has_side_effects=True, vmem_limit_bytes=60 * 1024 * 1024
        ),
        cost_estimate=pl.CostEstimate(flops=6_000_000_000, bytes_accessed=4_000_000, transcendentals=0),
    )(vectors, state_order)


def solution(mesh):
    return jax.shard_map(
        on_device,
        mesh=mesh,
        in_specs=(P("slab", "blk"), P("blk")),
        out_specs=P(None, "slab", "blk"),
        check_vma=False,
    )
```

time: 117 us -> 108 us (0.923)
  Pallas kernels: 116 us -> 107 us
    pallas_call x1, Pallas kernels: 116 us -> 107 us  [on_device(): pl.pallas_call(kernel, out_shape=jax.ShapeDtypeStruct((4, 12, SB), F32),...]
where the time goes in v3:
time: 108 us
  Pallas kernels  107 us (99%)
  local copies, waits for them, and re-layouts  1.56 us (1%)
    pallas_call x1, Pallas kernels, on_device(): pl.pallas_call(kernel, out_shape=jax.ShapeDtypeStruct((4, 12, SB), F32),...  107 us

profile of v3, /device:TPU:1, one launch (start us, length us, event | category | flops | bytes accessed | tf_op | source)
XLA Modules:
  0.0 108.2 jit_solution(12829816482449355968)
XLA Ops:
  0.0 106.6 %shard_map.28 = f32[4,12,384]{2,1,0:T(8,128)} custom-call(bf16[4608,384]{1,0:T(8,128)(2,1)} %vec_hbm.1, s32[384]{0:T(512)} %order.1), custom_call_target="tpu_custom_call" | custom-call | flops 6000000000 | bytes 4000000 | tf_op jit(solution)/shard_map/pallas_call | solution.py:442
  106.6 1.6 %copy.3 = f32[4,12,384]{2,0,1:T(4,128)} copy(f32[4,12,384]{2,1,0:T(8,128)} %shard_map.28) | data formatting | bytes 147456 | tf_op jit(solution)/shard_map/pallas_call | solution.py:442

commit v4 on v3

--- a/solution.py
+++ b/solution.py
@@ -15,12 +15,12 @@
 SENT = jnp.bfloat16
 MESH = pl.DeviceIdType.MESH
 NEIGHBOURS = (3, 1, 2)
-TILE = {(2, 0): 2, (2, 1): 3, (0, 0): 4, (0, 1): 5, (1, 0): 6, (1, 1): 7, (0, 2): 8, (1, 2): 9}
+TILE = {(0, 0): 2, (0, 1): 3, (1, 0): 4, (1, 1): 5, (0, 2): 6, (1, 2): 7, (2, 2): 8}
 
 
 def kernel(
     vec_hbm, order, out,
-    vec, w, u, halo, it, vn, whole, part, xrecv, zsend, zrecv, fin, finr,
+    vec, w, u, halo, it, vn, whole, part, xrecv, zsend, zrecv, fin, finr, layout,
     swap_s, swap_r, pair_s, pair_r, outer_s, outer_r, sib_s, sib_r,
     y1_s, y1_r, y2_s, y2_r, x_s, x_r, z_s, z_r, fin_s, fin_r, load, sent,
 ):
@@ -100,8 +100,12 @@
         remote(u.at[j, :, :, zl], halo.at[1 - zl, j], outer_s.at[j], outer_r.at[j], outer_dev)
         for j in range(3)
     ]
+    on = ((y + 2) % 4) // 2
     hop1 = [
-        [remote(u.at[j, d], vn.at[d, j], y1_s.at[d, j], y1_r.at[d, j], (up, down)[d]) for d in range(2)]
+        [
+            remote(u.at[j, d, half], vn.at[d, j, half], y1_s.at[d, j, part_], y1_r.at[d, j, part_], (up, down)[d])
+            for part_, half in enumerate((on, 1 - on)) for d in range(2)
+        ]
         for j in range(3)
     ]
     hu = (((y + 1) % 4) // 2, ((y + 3) % 4) // 2)
@@ -126,6 +130,7 @@
         dst = lax.broadcasted_iota(jnp.int32, (SB, SB), 1)
         slot = ((dst % PIECE) // 4) * 12 + (dst // PIECE) * 4 + dst % 4
         laid = jnp.where(slot == src, 1.0, 0.0).astype(BF16)
+        layout[...] = laid
         onehot = jnp.dot(picked, laid, preferred_element_type=F32).astype(BF16)
         fetch.wait()
 
@@ -163,18 +168,16 @@
         return jnp.concatenate([piece.reshape(CHUNK, PIECE) for piece in pieces], axis=1)
 
     def product(n, who, rows, cols):
-        def chunk(s, total):
-            if n == 0:
-                par, half = s // 2, s % 2
-                right = wide([u[j, par, half] for j in cols])
-            else:
-                par, half = {1: (1, s), 2: (s, y // 2), 3: (0, s)}[n]
-                right = wide([vn[NEIGHBOURS.index(n), j, s] for j in cols])
-            left = jnp.concatenate([it[who, i, par, half] for i in rows], axis=0)
-            return total + jnp.dot(left, right, preferred_element_type=F32)
-
-        zero = jnp.zeros((PIECE * len(rows), PIECE * len(cols)), F32)
-        return lax.fori_loop(0, 4 if n == 0 else 2, chunk, zero)
+        if n == 0:
+            steps = [(s // 2, s % 2) for s in range(4)]
+            right = [wide([u[j, par, half] for j in cols]) for par, half in steps]
+        else:
+            steps = [{1: (1, s), 2: (s, y // 2), 3: (0, s)}[n] for s in range(2)]
+            right = [wide([vn[NEIGHBOURS.index(n), j, s] for j in cols]) for s in range(2)]
+        left = [jnp.concatenate([it[who, i, par, half] for i in rows], axis=0) for par, half in steps]
+        return jnp.dot(
+            jnp.concatenate(left, axis=1), jnp.concatenate(right, axis=0), preferred_element_type=F32
+        )
 
     def kind(t):
         if t == 0:
@@ -186,7 +189,7 @@
         yp = jnp.where(matched, (y + n) % 4, y)
         return matched, zp, yp, jnp.where(matched, 4 - n, 3 + n)
 
-    def put(t, rows, cols, last):
+    def put(t, rows, cols, early):
         n = 0 if t == 0 else (t - 1) % 3 + 1
         got = product(n, c if t < 4 else 1 - c, rows, cols)
         matched = kind(t)[0]
@@ -197,7 +200,7 @@
                     tile = got[a * PIECE:(a + 1) * PIECE, b * PIECE:(b + 1) * PIECE]
                     at = (j, i) if swapped else (i, j)
                     tile = -tile.T if swapped else tile
-                    slot = last[int(swapped)] if at == (2, 2) else TILE[at]
+                    slot = TILE[at] if at in TILE else at[1] + (0 if early else 10)
                     whole[t, slot] = tile.reshape(4, 32, PIECE)
                     part[t, slot] = tile.reshape(4, 32, PIECE).astype(SENT)
 
@@ -228,21 +231,25 @@
         _, zp, yp, slot = kind(t)
         here = (zp == zl) & (yp == y) & keeper
         for h in range(4):
-            is_self = here & (zh == h)
-            share = total[:, 8 * h:8 * h + 8].reshape(8 * length, PIECE)
-
-            @pl.when(is_self)
-            def _():
-                zrecv[slot, z8, rows] = share
-
-            @pl.when(jnp.logical_not(is_self))
-            def _():
-                zsend[t, h, rows] = share
-                remote(zsend.at[t, h, rows], zrecv.at[slot, z8, rows], z_s.at[t], z_r.at[slot],
-                       dev(x, h, zp, zp, yp)).start()
+            zsend[t, h, rows] = total[:, 8 * h:8 * h + 8].reshape(8 * length, PIECE)
+            copy = remote(zsend.at[t, h, rows], zrecv.at[slot, z8, rows], z_s.at[t], z_r.at[slot], dev(x, h, zp, zp, yp))
+            pl.when(jnp.logical_not(here & (zh == h)))(copy.start)
+
+        @pl.when(here)
+        def _():
+            zrecv[slot, z8, rows] = zsend[t, zh, rows]
 
     def side(t, one, other):
         return jnp.where(kind(t)[0], one, other)
+
+    def pass_on(j):
+        for d in range(2):
+            hop1[j][d].wait_recv()
+            hop2[j][d].start()
+
+    def all_here(j):
+        arrive(hop1[j][2:])
+        arrive(hop2[j])
 
     def settle(copies):
         for copy in copies:
@@ -282,8 +289,7 @@
         pairs[0].wait_send()
         pl.semaphore_signal(sent, inc=1, device_id=sibling, device_id_type=MESH)
         for j in range(3):
-            arrive(hop1[j])
-            go(hop2[j])
+            pass_on(j)
 
         def ready(j):
             arrive([pairs[j], outers[j]])
@@ -292,19 +298,19 @@
 
         ready(0)
         for j in range(3):
-            arrive(hop2[j])
+            all_here(j)
         pl.semaphore_wait(sent, 1)
         pairs[1].start()
         ready(1)
-        runs = [(t, 0, side(t, 4, 2), 6) for t in range(7)]
-        rest = [(t, 1, side(t, 0, 8), 4) for t in range(7)]
+        runs = [(t, 0, side(t, 2, 0), 6) for t in range(7)]
+        rest = [(t, 1, side(t, 8, 6), 4) for t in range(7)]
 
         def early(t):
-            put(t, (0, 1), everything, (0, 0))
+            put(t, (0, 1), everything, True)
             go(xcopies(*runs[t]))
 
         def late(t):
-            put(t, (2,), everything, (0, 10))
+            put(t, (2,), everything, False)
             go(xcopies(*rest[t]))
 
         for t in range(4):
@@ -345,21 +351,28 @@
             def _():
                 pltpu.make_async_copy(zrecv.at[s, :, 0:80], zrecv.at[s, :, 0:80], z_r.at[s]).wait()
 
-        src = lax.broadcasted_iota(jnp.int32, (SB, SB), 0)
-        dst = lax.broadcasted_iota(jnp.int32, (SB, SB), 1)
-        unsort = jnp.where(((src % PIECE) // 4) * 12 + (src // PIECE) * 4 + src % 4 == dst, 1.0, 0.0).astype(F32)
+        flats = []
         for k in range(4):
             total = jnp.sum(zrecv[k].astype(F32), axis=0)
             if k > 0:
                 total = total + jnp.sum(zrecv[3 + k].astype(F32), axis=0)
             at = [total[8 * i:8 * i + 8] for i in range(12)]
-            flat = jnp.concatenate([
-                jnp.concatenate([at[4], at[5], at[8]], axis=1),
-                jnp.concatenate([at[6], at[7], at[9]], axis=1),
-                jnp.concatenate([at[2], at[3], at[0] + at[10]], axis=1),
-            ], axis=0)
-            flat = jnp.dot(flat, unsort, precision=lax.Precision.HIGHEST, preferred_element_type=F32)
-            fin[k] = flat.reshape(3, 8, SB)
+            flats += [
+                jnp.concatenate([at[2], at[3], at[6]], axis=1),
+                jnp.concatenate([at[4], at[5], at[7]], axis=1),
+                jnp.concatenate([at[0] + at[10], at[1] + at[11], at[8]], axis=1),
+            ]
+        flat = jnp.concatenate(flats, axis=0)
+        high = flat.astype(BF16)
+        left = flat - high.astype(F32)
+        middle = left.astype(BF16)
+        low = (left - middle.astype(F32)).astype(BF16)
+        flat = lax.dot_general(
+            jnp.concatenate([high, middle, low], axis=0), layout[...], (((1,), (1,)), ((), ())),
+            preferred_element_type=F32,
+        )
+        flat = flat[0:96] + flat[96:192] + flat[192:288]
+        fin[...] = flat.reshape(4, 3, 8, SB)
         final.start()
         write(fin)
         final.wait_send()
@@ -383,50 +396,44 @@
         go(hop1[0])
         outers[0].start()
         ready(0)
+        pass_on(0)
         swaps[1].wait_send()
         swaps[1].wait_recv()
         go(hop1[1])
         outers[1].start()
-        arrive(hop1[0])
-        go(hop2[0])
+        pass_on(1)
         swaps[2].wait_send()
         pl.semaphore_signal(sent, inc=1, device_id=sibling, device_id_type=MESH)
         swaps[2].wait_recv()
         go(hop1[2])
         outers[2].start()
-        arrive(hop1[1])
-        go(hop2[1])
-        arrive(hop2[0])
-        arrive(hop2[1])
+        pass_on(2)
+        all_here(0)
+        all_here(1)
+        runs = [(t, 0, 2, 4) for t in range(4)] + [(t, 0, side(t, 0, 2), 6) for t in (4, 5, 6)]
+        ready(1)
+        for t in range(4):
+            put(t, (0, 1), (0, 1), True)
+            go(xcopies(*runs[t]))
         arrive(sib)
-        runs = [(t, 0, 4, 4) for t in range(4)] + [(t, 0, side(t, 2, 4), 6) for t in (4, 5, 6)]
-        for t in (4, 5, 6):
-            put(t, everything, (0, 1), (0, 0))
+        for t in (4, 5, 6):
+            put(t, everything, (0, 1), True)
             go(xcopies(*runs[t]))
-        arrive(hop1[2])
-        go(hop2[2])
-        ready(1)
-        for t in range(4):
-            put(t, (0, 1), (0, 1), (0, 0))
-            go(xcopies(*runs[t]))
-        for t in (4, 5, 6):
+        for t in range(4):
             collect(*runs[t])
-        arrive(hop2[2])
+        all_here(2)
         rest = []
         for t in (4, 5, 6):
-            put(t, everything, (2,), (10, 0))
-            rest.append((t, 1, side(t, 8, 0), 4))
+            put(t, everything, (2,), False)
+            rest.append((t, 1, side(t, 6, 8), 4))
             go(xcopies(*rest[-1]))
         ready(2)
         for t in range(4):
-            put(t, (2,), everything, (0, 0))
-            put(t, (0, 1), (2,), (0, 0))
-            rest += [(t, 1, 0, 4), (t, 2, 8, 2)]
-            go(xcopies(*rest[-2]))
+            put(t, (2,), everything, False)
+            put(t, (0, 1), (2,), False)
+            rest.append((t, 1, 6, 6))
             go(xcopies(*rest[-1]))
-        for t in range(4):
-            collect(*runs[t])
-        for run in rest:
+        for run in runs[4:] + rest:
             collect(*run)
         settle(pairs)
         done(runs + rest)
@@ -458,9 +465,10 @@
             pltpu.VMEM((7, 8, 96, PIECE), SENT),
             pltpu.VMEM((4, 3, 8, SB), F32),
             pltpu.VMEM((4, 3, 8, SB), F32),
+            pltpu.VMEM((SB, SB), BF16),
             dma((3,)), dma((3,)), dma((3,)), dma((3,)), dma((3,)), dma((3,)),
             dma((3,)), dma((3,)),
-            dma((2, 3)), dma((2, 3)), dma((2, 3)), dma((2, 3)),
+            dma((2, 3, 2)), dma((2, 3, 2)), dma((2, 3)), dma((2, 3)),
             dma((7, 3, 3)), dma((7, 3, 3)), dma((7,)), dma((7,)),
             dma, dma, dma, pltpu.SemaphoreType.REGULAR,
         ],

time: 108 us -> 104 us (0.963)
  Pallas kernels: 107 us -> 102 us
    pallas_call x1, Pallas kernels: 107 us -> 102 us  [on_device(): pl.pallas_call(kernel, out_shape=jax.ShapeDtypeStruct((4, 12, SB), F32),...]
where the time goes in v4:
time: 104 us
  Pallas kernels  102 us (98%)
  local copies, waits for them, and re-layouts  1.56 us (2%)
    pallas_call x1, Pallas kernels, on_device(): pl.pallas_call(kernel, out_shape=jax.ShapeDtypeStruct((4, 12, SB), F32),...  102 us

profile of v4, /device:TPU:1, one launch (start us, length us, event | category | flops | bytes accessed | tf_op | source)
XLA Modules:
  0.0 103.7 jit_solution(765584673875999023)
XLA Ops:
  0.0 102.2 %shard_map.28 = f32[4,12,384]{2,1,0:T(8,128)} custom-call(bf16[4608,384]{1,0:T(8,128)(2,1)} %vec_hbm.1, s32[384]{0:T(512)} %order.1), custom_call_target="tpu_custom_call" | custom-call | flops 6000000000 | bytes 4000000 | tf_op jit(solution)/shard_map/pallas_call | solution.py:449
  102.2 1.6 %copy.3 = f32[4,12,384]{2,0,1:T(4,128)} copy(f32[4,12,384]{2,1,0:T(8,128)} %shard_map.28) | data formatting | bytes 147456 | tf_op jit(solution)/shard_map/pallas_call | solution.py:449

commit v5 on v4

--- a/solution.py
+++ b/solution.py
@@ -134,21 +134,25 @@
         onehot = jnp.dot(picked, laid, preferred_element_type=F32).astype(BF16)
         fetch.wait()
 
+    def sort(j, kept):
         def sort_chunk(i, carry):
             plane, q = i // 4, i % 4
             at = pl.multiple_of(i * QUARTER, QUARTER)
-            got = jnp.dot(vec[pl.ds(at, QUARTER), :], onehot, preferred_element_type=F32).astype(BF16)
-            for j in range(3):
-                w[j, q % 2, q // 2, plane] = got[:, j * PIECE:(j + 1) * PIECE]
-
-            @pl.when(keeper)
-            def _():
-                for j in range(3):
-                    u[j, q % 2, q // 2, plane] = got[:, j * PIECE:(j + 1) * PIECE]
-
+            got = jnp.dot(
+                vec[pl.ds(at, QUARTER), :], onehot[:, j * PIECE:(j + 1) * PIECE], preferred_element_type=F32
+            ).astype(BF16)
+            w[j, q % 2, q // 2, plane] = got
+
+            def keep_it():
+                u[j, q % 2, q // 2, plane] = got
+
+            pl.when(kept)(keep_it)
             return carry
 
         lax.fori_loop(0, 8, sort_chunk, 0)
+
+    with jax.named_scope("sort"):
+        sort(0, keeper)
     pl.semaphore_wait(barrier, jnp.where(keeper, 43, 27))
 
     def image(lo, hi):
@@ -284,8 +288,10 @@
         everything = (0, 1, 2)
         pairs[0].start()
         for j in range(3):
+            if j > 0:
+                sort(j, True)
             go(hop1[j])
-        go(outers)
+            outers[j].start()
         pairs[0].wait_send()
         pl.semaphore_signal(sent, inc=1, device_id=sibling, device_id_type=MESH)
         for j in range(3):
@@ -386,8 +392,11 @@
             image(j, j + 1)
             sib[j].start()
 
-        go(pairs)
         swaps[0].start()
+        pairs[0].start()
+        for j in (1, 2):
+            sort(j, False)
+            pairs[j].start()
         pl.semaphore_wait(sent, 1)
         swaps[1].start()
         swaps[0].wait_send()

time: 104 us -> 103 us (level)
    pallas_call x1, Pallas kernels: 102 us -> 101 us  [on_device(): pl.pallas_call(kernel, out_shape=jax.ShapeDtypeStruct((4, 12, SB), F32),...]
where the time goes in v5:
time: 103 us; the launch traced here: 102 us
  Pallas kernels  101 us (98%)
  local copies, waits for them, and re-layouts  1.56 us (2%)
    pallas_call x1, Pallas kernels, on_device(): pl.pallas_call(kernel, out_shape=jax.ShapeDtypeStruct((4, 12, SB), F32),...  101 us

profile of v5, /device:TPU:1, one launch (start us, length us, event | category | flops | bytes accessed | tf_op | source)
XLA Modules:
  0.0 102.4 jit_solution(9095689533239666494)
XLA Ops:
  0.0 100.9 %shard_map.28 = f32[4,12,384]{2,1,0:T(8,128)} custom-call(bf16[4608,384]{1,0:T(8,128)(2,1)} %vec_hbm.1, s32[384]{0:T(512)} %order.1), custom_call_target="tpu_custom_call" | custom-call | flops 6000000000 | bytes 4000000 | tf_op jit(solution)/shard_map/pallas_call | solution.py:458
  100.9 1.6 %copy.3 = f32[4,12,384]{2,0,1:T(4,128)} copy(f32[4,12,384]{2,1,0:T(8,128)} %shard_map.28) | data formatting | bytes 147456 | tf_op jit(solution)/shard_map/pallas_call | solution.py:458

commit v6 on v5

--- a/solution.py
+++ b/solution.py
@@ -45,8 +45,12 @@
     down = dev(x, zh, c, zl, (y + 3) % 4)
     sibling = dev(x, zh, 1 - c, zl, y)
 
-    fetch = pltpu.make_async_copy(vec_hbm, vec, load)
-    fetch.start()
+    fetch = [
+        pltpu.make_async_copy(vec_hbm.at[pl.ds(f * CHUNK, CHUNK)], vec.at[pl.ds(f * CHUNK, CHUNK)], load.at[f])
+        for f in range(4)
+    ]
+    for copy in fetch:
+        copy.start()
     zrecv[:, :, 0:16] = jnp.zeros((7, 8, 16, PIECE), SENT)
     zrecv[:, :, 80:96] = jnp.zeros((7, 8, 16, PIECE), SENT)
     barrier = pltpu.get_barrier_semaphore()
@@ -132,7 +136,6 @@
         laid = jnp.where(slot == src, 1.0, 0.0).astype(BF16)
         layout[...] = laid
         onehot = jnp.dot(picked, laid, preferred_element_type=F32).astype(BF16)
-        fetch.wait()
 
     def sort(j, kept):
         def sort_chunk(i, carry):
@@ -149,7 +152,10 @@
             pl.when(kept)(keep_it)
             return carry
 
-        lax.fori_loop(0, 8, sort_chunk, 0)
+        for f in range(4):
+            if j == 0:
+                fetch[f].wait()
+            lax.fori_loop(2 * f, 2 * f + 2, sort_chunk, 0)
 
     with jax.named_scope("sort"):
         sort(0, keeper)
@@ -479,7 +485,7 @@
             dma((3,)), dma((3,)),
             dma((2, 3, 2)), dma((2, 3, 2)), dma((2, 3)), dma((2, 3)),
             dma((7, 3, 3)), dma((7, 3, 3)), dma((7,)), dma((7,)),
-            dma, dma, dma, pltpu.SemaphoreType.REGULAR,
+            dma, dma, dma((4,)), pltpu.SemaphoreType.REGULAR,
         ],
         compiler_params=pltpu.CompilerParams(
             collective_id=0, has_side_effects=True, vmem_limit_bytes=60 * 1024 * 1024

time: 103 us -> 102 us (level)
  no operation moved by 1% of the time
where the time goes in v6:
time: 102 us
  Pallas kernels  101 us (99%)
  local copies, waits for them, and re-layouts  1.56 us (2%)
    pallas_call x1, Pallas kernels, on_device(): pl.pallas_call(kernel, out_shape=jax.ShapeDtypeStruct((4, 12, SB), F32),...  101 us

profile of v6, /device:TPU:1, one launch (start us, length us, event | category | flops | bytes accessed | tf_op | source)
XLA Modules:
  0.0 102.1 jit_solution(3134960973126925515)
XLA Ops:
  0.0 100.6 %shard_map.28 = f32[4,12,384]{2,1,0:T(8,128)} custom-call(bf16[4608,384]{1,0:T(8,128)(2,1)} %vec_hbm.1, s32[384]{0:T(512)} %order.1), custom_call_target="tpu_custom_call" | custom-call | flops 6000000000 | bytes 4000000 | tf_op jit(solution)/shard_map/pallas_call | solution.py:464
  100.6 1.6 %copy.3 = f32[4,12,384]{2,0,1:T(4,128)} copy(f32[4,12,384]{2,1,0:T(8,128)} %shard_map.28) | data formatting | bytes 147456 | tf_op jit(solution)/shard_map/pallas_call | solution.py:464
